TPU v7x, 32 devices: a whole 2x2x4 slice. The times are simulated.
32 devices in a mesh: rep: 2 (over x), patch: 8 (over z, y), grp: 2 (over core).
Axes of the slice: x: 2, y: 2, z: 4, core: 2. Of those that a mesh axis runs over, the one named last changes fastest.
Arguments:
- queries: bfloat16 [2560, 1536], P(('rep', 'patch', 'grp')), parts along dimension 0, may hold values from -6 to 6
- keys: bfloat16 [2560, 1536], P(('rep', 'patch', 'grp')), parts along dimension 0, may hold values from -6 to 6
- values: bfloat16 [2560, 1536], P(('rep', 'patch', 'grp')), parts along dimension 0, may hold values from -6 to 6
- stale_keys: bfloat16 [2560, 1536], P(('rep', 'patch', 'grp')), parts along dimension 0, may hold values from -4 to 4
- stale_values: bfloat16 [2560, 1536], P(('rep', 'patch', 'grp')), parts along dimension 0, may hold values from -6 to 6
- q_gain: float32 [128], replicated, may hold values from 1 to 3
- k_gain: float32 [128], replicated, may hold values from 1 to 3
- o_weight: bfloat16 [1536, 3072], replicated, may hold values from -0.15625 to 0.15625
- slot_positions: int32 [2560], P('rep'), parts along dimension 0, may hold values from 0 to 1279, each once
Outputs:
- attended: bfloat16 [2560, 3072], P(('rep', 'patch', 'grp')), parts along dimension 0
There are 2 independent parts, one for each index of `rep`. A program takes and returns all parts, laid end to end along the dimension named above; an argument that names none is the same for every part. Nothing has to cross between parts.
Inputs may be any that keep to these rules, and one draw needn't show every extreme that they name: `slot_positions`: a permutation of the slots' patch positions; positions 1275 and above mark padding.
All inputs are finite; a program needn't handle non-finite values.
Results may differ from a plain program's by a relative error of at most 0.012.
Values may be sent and summed in bfloat16 or wider, within the bound.
A program may use at most 192 MiB of HBM per device.

v0:
```python
import jax
import jax.numpy as jnp
from jax import lax
from jax.sharding import PartitionSpec as P

LAT_H = 34
LAT_W = 60


def partner_2(value, axis, apart):
    mask = 2**apart
    pairs = [(source, source ^ mask) for source in range(lax.axis_size(axis))]
    return lax.ppermute(value, axis, pairs)


def rotary(rows_f, pos_ids):
    head_dim = rows_f.shape[-1]
    per_frame = LAT_H * LAT_W
    frame_pos = (pos_ids // per_frame).astype(jnp.float32)
    row_pos = (pos_ids // LAT_W % LAT_H).astype(jnp.float32)
    col_pos = (pos_ids % LAT_W).astype(jnp.float32)
    pieces_out = []
    offset_at = 0
    for coord_pos, width in (
        (frame_pos, head_dim // 8),
        (row_pos, 7 * head_dim // 16),
        (col_pos, 7 * head_dim // 16),
    ):
        half_width = width // 2
        frequency = 256.0 ** (-jnp.arange(half_width, dtype=jnp.float32) * 2.0 / width)
        angles = coord_pos[:, None] * frequency[None, :]
        cosine = jnp.cos(angles)[:, None, :]
        sine = jnp.sin(angles)[:, None, :]
        first_half = rows_f[..., offset_at : offset_at + half_width]
        second_half = rows_f[..., offset_at + half_width : offset_at + width]
        pieces_out.append(first_half * cosine - second_half * sine)
        pieces_out.append(first_half * sine + second_half * cosine)
        offset_at = offset_at + width
    return jnp.concatenate(pieces_out, axis=-1)


def prepare(projected, gain, pos_ids):
    row_count = projected.shape[0]
    head_dim = gain.shape[0]
    rows_f = projected.astype(jnp.float32).reshape(row_count, -1, head_dim)
    mean_sq = jnp.mean(rows_f * rows_f, axis=-1, keepdims=True)
    normed = rows_f * lax.rsqrt(mean_sq + 1e-06) * gain
    return rotary(normed, pos_ids).astype(jnp.bfloat16)


def body(queries, keys, values, stale_keys, stale_values, q_gain, k_gain, o_weight, slot_positions):
    row_count = queries.shape[0]
    head_dim = q_gain.shape[0]
    head_count = queries.shape[1] // head_dim
    seq_len = slot_positions.shape[0]
    live_count = seq_len - max(seq_len // 256, 2)
    my_side = lax.axis_index("grp")
    my_block = lax.axis_index("patch") * 2 + my_side
    own_pos = lax.dynamic_slice_in_dim(slot_positions, my_block * row_count, row_count)
    q_rot = prepare(queries, q_gain, own_pos)
    inv_root = 1.0 / head_dim**0.5

    def attend(state, portion, key_side):
        count = portion.shape[1]
        gathered_idx = jnp.arange(count, dtype=jnp.int32)
        slot_idx = (gathered_idx // row_count * 2 + key_side) * row_count + gathered_idx % row_count
        key_live = jnp.take(slot_positions, slot_idx) < live_count
        key_rows = portion[0].reshape(count, head_count, head_dim)
        value_rows = portion[1].reshape(count, head_count, head_dim)
        scores = (
            jnp.einsum("qhd,khd->hqk", q_rot, key_rows, preferred_element_type=jnp.float32)
            * inv_root
        )
        scores = jnp.where(key_live[None, None, :], scores, -1e30)
        run_max, run_sum, run_acc = state
        new_max = jnp.maximum(run_max, jnp.max(scores, axis=2))
        fade = jnp.exp(run_max - new_max)
        probs = jnp.exp(scores - new_max[:, :, None])
        new_sum = run_sum * fade + jnp.sum(probs, axis=2)
        added = jnp.einsum(
            "hqk,khd->hqd",
            probs.astype(jnp.bfloat16),
            value_rows,
            preferred_element_type=jnp.float32,
        )
        return (new_max, new_sum, run_acc * fade[:, :, None] + added)

    start_state = (
        jnp.full((head_count, row_count), -1e30, jnp.float32),
        jnp.zeros((head_count, row_count), jnp.float32),
        jnp.zeros((head_count, row_count, head_dim), jnp.float32),
    )
    stale_stack = jnp.stack([stale_keys, stale_values])
    partner = partner_2(stale_stack, "grp", 0)
    state = attend(start_state, lax.all_gather(partner, "patch", axis=1, tiled=True), 1 - my_side)
    k_rot = prepare(keys, k_gain, own_pos).reshape(row_count, head_count * head_dim)
    state = attend(
        state, lax.all_gather(jnp.stack([k_rot, values]), "patch", axis=1, tiled=True), my_side
    )
    run_max, run_sum, run_acc = state
    per_head = run_acc / run_sum[:, :, None]
    attn = (
        per_head.transpose(1, 0, 2).reshape(row_count, head_count * head_dim).astype(jnp.bfloat16)
    )
    projected = jnp.dot(attn, o_weight, preferred_element_type=jnp.float32)
    own_live = own_pos < live_count
    return jnp.where(own_live[:, None], projected, 0.0).astype(jnp.bfloat16)


def solution(mesh):
    in_specs = (
        P(("rep", "patch", "grp"), None),
        P(("rep", "patch", "grp"), None),
        P(("rep", "patch", "grp"), None),
        P(("rep", "patch", "grp"), None),
        P(("rep", "patch", "grp"), None),
        P(),
        P(),
        P(),
        P("rep"),
    )
    out_specs = P(("rep", "patch", "grp"), None)
    return jax.shard_map(body, mesh=mesh, in_specs=in_specs, out_specs=out_specs, check_vma=False)
```

profile of v0, /device:TPU:14, one launch (start us, length us, event | category | flops | bytes accessed | tf_op | source)
XLA Modules:
  0.0 197.0 jit_solution(4198115461739227899)
XLA Ops:
  6.6 1.3 reshape.235
  7.9 0.2 multiply_reduce_fusion
  8.3 1.1 reshape.233
  9.4 0.2 multiply_reduce_fusion.1
  10.1 0.4 multiply_cosine_fusion
  10.5 0.3 fusion.43
  10.9 0.4 add_convert_fusion.2
  11.3 0.6 add_convert_fusion
  11.9 0.7 concatenate.9
  12.9 0.9 pad_maximum_fusion.1
  13.8 0.2 all-gather.3.cloned.1.call-start
  14.2 1.9 collective-permute-done
  16.0 1.3 copy.41
  17.4 3.9 %gather_fusion = s32[640]{0:T(1024)S(1)} fusion(s32[1280]{0:T(1024)S(1)} %copy-done, s32[1024]{0:T(1024)S(1)} %pad_clamp_fusion.1), kind=kCustom, calls=%fused_computation.clone | custom fusion | bytes 7680 | tf_op jit(solution)/shard_map/jit(_take)/gather | solution.py:67
  21.3 3.9 %gather_fusion.1 = s32[640]{0:T(1024)S(1)} fusion(s32[1280]{0:T(1024)S(1)} %copy-done, s32[1024]{0:T(1024)S(1)} %pad_clamp_fusion), kind=kCustom, calls=%fused_computation.1.clone | custom fusion | bytes 7680 | tf_op jit(solution)/shard_map/jit(_take)/gather | solution.py:67
  25.1 0.6 add_convert_fusion.3
  25.7 1.3 concatenate.8
  27.1 56.6 %all-gather.5.cloned.1.call-done = bf16[2,640,1536]{2,1,0:T(8,128)(2,1)} async-done(((bf16[2,80,1536]{2,1,0:T(8,128)(2,1)}), bf16[2,640,1536]{2,1,0:T(8,128)(2,1)}) %all-gather.5.cloned.1.call-update) | async-done | bytes 3932176 | tf_op jit(solution)/shard_map/all_gather | solution.py:98
  83.7 3.7 %fusion.70 = (bf16[1,640,1536]{2,1,0:T(8,128)(2,1)S(1)}, bf16[1,640,1536]{2,1,0:T(8,128)(2,1)}) fusion(bf16[2,640,1536]{2,1,0:T(8,128)(2,1)} %all-gather.5.cloned.1.call-done), kind=kLoop, calls=%fused_computation.108 | loop fusion | bytes 7864320 | tf_op jit(solution)/shard_map/slice | solution.py:69
  87.5 4.0 %copy.49 = bf16[1,640,1536]{1,2,0:T(8,128)(2,1)} copy(bf16[1,640,1536]{2,1,0:T(8,128)(2,1)} %get-tuple-element.11) | data formatting | bytes 3932160 | tf_op jit(solution)/shard_map/slice | solution.py:68
  91.4 2.3 %copy.51 = bf16[1,640,1536]{1,2,0:T(8,128)(2,1)} copy(bf16[1,640,1536]{2,1,0:T(8,128)(2,1)S(1)} %get-tuple-element.10) | data formatting | bytes 3932160 | tf_op jit(solution)/shard_map/slice | solution.py:69
  93.7 2.4 %fusion.2 = (f32[12,80]{1,0:T(8,128)S(1)}, f32[12,80,640]{2,1,0:T(8,128)S(1)}) fusion(pred[640]{0:T(1024)(128)(4,1)S(1)} %select_compare_fusion, bf16[80,12,128]{2,0,1:T(8,128)(2,1)} %concatenate.8, bf16[640,12,128]{0,2,1:T(8,128)(2,1)} %bitcast.72), kind=kOutput, calls=%fused_computation.9 | convolution fusion | flops 159128640 | bytes 4673920 | tf_op jit(solution)/shard_map/qhd,khd->hqk/dot_general | solution.py:71
  96.1 58.3 %all-gather.3.cloned.1.call-done = bf16[2,640,1536]{2,0,1:T(2,128)(2,1)} async-done(((bf16[2,80,1536]{2,0,1:T(2,128)(2,1)}), bf16[2,640,1536]{2,0,1:T(2,128)(2,1)}) %all-gather.3.cloned.1.call-update) | async-done | bytes 3932176 | tf_op jit(solution)/shard_map/all_gather | solution.py:95
  154.4 9.5 %fusion.71 = (bf16[1,640,1536]{2,0,1:T(2,128)(2,1)}, bf16[1,640,1536]{2,0,1:T(2,128)(2,1)}) fusion(bf16[2,640,1536]{2,0,1:T(2,128)(2,1)} %all-gather.3.cloned.1.call-done), kind=kLoop, calls=%fused_computation.109 | loop fusion | bytes 7864320 | tf_op jit(solution)/shard_map/slice | solution.py:68
  163.9 8.6 %copy.59 = bf16[1,640,1536]{1,2,0:T(8,128)(2,1)} copy(bf16[1,640,1536]{2,0,1:T(2,128)(2,1)} %get-tuple-element.13) | data formatting | bytes 3932160
  172.5 8.7 %copy.58 = bf16[1,640,1536]{1,2,0:T(8,128)(2,1)} copy(bf16[1,640,1536]{2,0,1:T(2,128)(2,1)} %get-tuple-element.12) | data formatting | bytes 3932160
  181.2 2.5 %fusion.1 = (f32[12,80]{1,0:T(8,128)S(1)}, f32[12,80,640]{2,1,0:T(8,128)S(1)}) fusion(pred[640]{0:T(1024)(128)(4,1)S(1)} %select_compare_fusion.1, bf16[80,12,128]{2,0,1:T(8,128)(2,1)} %concatenate.8, bf16[640,12,128]{0,2,1:T(8,128)(2,1)} %bitcast.73), kind=kOutput, calls=%fused_computation.8 | convolution fusion | flops 159128640 | bytes 4673920 | tf_op jit(solution)/shard_map/qhd,khd->hqk/dot_general | solution.py:71
  183.6 0.8 fusion.5
  184.4 0.8 fusion.3
  185.2 1.1 fusion.31
  186.4 1.1 fusion.40
  187.5 2.6 %fusion = bf16[80,3072]{1,0:T(8,128)(2,1)} fusion(bf16[1536,3072]{1,0:T(8,128)(2,1)S(1)} %bitcast.71, pred[80]{0:T(512)(128)(4,1)S(1)} %broadcast_compare_fusion, bf16[12,10,8,128]{3,2,1,0:T(8,128)(2,1)S(1)} %fusion.40), kind=kOutput, calls=%fused_computation.3 | convolution fusion | flops 755466240 | bytes 10174544 | tf_op jit(solution)/shard_map/dot_general | solution.py:105
  (54 shorter events, 1.2 us)
Async XLA Ops:
  6.5 4.0 %copy-start.3 = (bf16[80,1536]{1,0:T(8,128)(2,1)S(1)}, bf16[80,1536]{1,0:T(8,128)(2,1)}, u32[]{:S(2)}) copy-start(bf16[80,1536]{1,0:T(8,128)(2,1)} %param.12) | copy-start | bytes 737284
  6.5 4.0 %copy-start.4 = (bf16[80,1536]{1,0:T(8,128)(2,1)S(1)}, bf16[80,1536]{1,0:T(8,128)(2,1)}, u32[]{:S(2)}) copy-start(bf16[80,1536]{1,0:T(8,128)(2,1)} %param.11) | copy-start | bytes 737284
  6.5 3.2 %copy-start = (s32[1280]{0:T(1024)S(1)}, s32[1280]{0:T(1024)}, u32[]{:S(2)}) copy-start(s32[1280]{0:T(1024)} %param.19) | copy-start | bytes 15364
  6.5 4.0 %copy-start.8 = (f32[128]{0:T(128)S(1)}, f32[128]{0:T(128)}, u32[]{:S(2)}) copy-start(f32[128]{0:T(128)} %param.17) | copy-start | bytes 1540
  6.5 4.0 %copy-start.9 = (f32[128]{0:T(128)S(1)}, f32[128]{0:T(128)}, u32[]{:S(2)}) copy-start(f32[128]{0:T(128)} %param.16) | copy-start | bytes 1540
  6.5 77.2 %all-gather.5.cloned.1.call-start = ((), (), s32[]{:S(2)}) async-start(), calls=%async_computation.1 | async-start | bytes 4423680 | tf_op jit(solution)/shard_map/all_gather | solution.py:98
  11.3 1.6 copy-start.5
  11.9 2.1 %copy-start.6 = (bf16[80,1536]{1,0:T(8,128)(2,1)S(1)}, bf16[80,1536]{1,0:T(8,128)(2,1)}, u32[]{:S(2)}) copy-start(bf16[80,1536]{1,0:T(8,128)(2,1)} %param.15) | copy-start | bytes 737284
  12.6 1.4 copy-start.7
  13.8 140.6 %all-gather.3.cloned.1.call-start = ((), (), s32[]{:S(2)}) async-start(), calls=%async_computation | async-start | bytes 4423680 | tf_op jit(solution)/shard_map/all_gather | solution.py:95
  14.1 1.9 collective-permute-start
  172.5 15.0 %slice-start = ((s8[9437184]{0:T(1024)(128)(4,1)}), s8[1048576]{0:T(1024)(128)(4,1)S(1)}, s32[]{:S(2)}) async-start(s8[9437184]{0:T(1024)(128)(4,1)} %bitcast.70), calls=%async_computation.2 | async-start | bytes 2097152
  181.2 6.4 %slice-start.1 = ((s8[9437184]{0:T(1024)(128)(4,1)}), s8[4194304]{0:T(1024)(128)(4,1)S(1)}, s32[]{:S(2)}) async-start(s8[9437184]{0:T(1024)(128)(4,1)} %bitcast.70), calls=%async_computation.3 | async-start | bytes 8388608
  183.6 1.6 copy-start.2
  184.4 2.0 copy-start.1
  185.2 2.3 %slice-start.2 = ((s8[9437184]{0:T(1024)(128)(4,1)}), s8[4194304]{0:T(1024)(128)(4,1)S(1)}, s32[]{:S(2)}) async-start(s8[9437184]{0:T(1024)(128)(4,1)} %bitcast.70), calls=%async_computation.4 | async-start | bytes 8388608
Sparse Core Ops, SparseCore 0:
  13.9 69.7 all-gather.4
  85.9 68.4 all-gather.2
where the time goes:
time: 201 us; the launch traced here: 197 us
  waiting for transfers between devices  117 us (58%)
  local copies, waits for them, and re-layouts  50.8 us (25%)
  between operations  13.8 us (7%)
  matrix products  9.73 us (5%)
  other arithmetic  5.57 us (3%)
    all_gather x1, waiting for transfers between devices, body(): lax.all_gather(partner, 'patch', axis=1, tiled=True)  58.3 us
    all_gather x1, waiting for transfers between devices, body(): lax.all_gather(jnp.stack([k_rot, values]), 'patch', axis=1, tiled=True)  56.6 us
    unnamed x28, local copies, waits for them, and re-layouts  17.3 us
    slice x2, local copies, waits for them, and re-layouts, attend(): key_rows = portion[0].reshape(count, head_count, head_dim)  13.4 us
    gather x2, local copies, waits for them, and re-layouts, attend(): key_live = jnp.take(slot_positions, slot_idx) < live_count  7.72 us
    slice x2, local copies, waits for them, and re-layouts, attend(): value_rows = portion[1].reshape(count, head_count, head_dim)  6 us
    dot_general x2, matrix products, attend(): jnp.einsum('qhd,khd->hqk', q_rot, key_rows, preferred_element_type=jnp.fl...  4.86 us
  transfers between devices with their start and end apart: 3, of which 3 were waited for; matrix products, arithmetic and copies ran while one was open for 12% of the time, Pallas kernels for 0%

commit v1 on v0

v1 whole, which is shorter than its diff:
```python
import functools

import jax
import jax.numpy as jnp
import numpy as np
from jax import lax
from jax.experimental import pallas as pl
from jax.experimental.pallas import tpu as pltpu
from jax.sharding import PartitionSpec as P

LAT_H = 34
LAT_W = 60
GROUPS = 4
MESH = pl.DeviceIdType.MESH


def swap_lanes(head_dim):
    order = []
    at = 0
    for width in (head_dim // 8, 7 * head_dim // 16, 7 * head_dim // 16):
        half = width // 2
        order += list(range(at + half, at + width)) + list(range(at, at + half))
        at += width
    return np.array(order)


def tables(pos_ids, head_dim):
    per_frame = LAT_H * LAT_W
    coords = (pos_ids // per_frame, pos_ids // LAT_W % LAT_H, pos_ids % LAT_W)
    freq = []
    which = []
    sign = []
    for idx, width in enumerate((head_dim // 8, 7 * head_dim // 16, 7 * head_dim // 16)):
        half = width // 2
        f = np.float32(256.0) ** (-np.arange(half, dtype=np.float32) * np.float32(2.0) / np.float32(width))
        freq += list(f) + list(f)
        which += [idx] * width
        sign += [-1.0] * half + [1.0] * half
    freq = jnp.asarray(np.array(freq, np.float32))[None, :]
    which = np.array(which)[None, :]
    sign = jnp.asarray(np.array(sign, np.float32))[None, :]
    f_pos, r_pos, c_pos = (x.astype(jnp.float32)[:, None] for x in coords)
    coord = jnp.where(which == 0, f_pos, jnp.where(which == 1, r_pos, c_pos))
    angles = coord * freq
    return jnp.cos(angles), jnp.sin(angles) * sign


def kernel(
    n_patch, heads, head_dim, rows,
    q_ref, k_ref, v_ref, sk_ref, sv_ref, tab_ref, perm_ref, bias_ref,
    out_ref,
    qrot, krot, qbuf, kv, osend, obuf,
    q_ssem, kv_ssem, f_ssem, o_ssem, q_rsem, kv_rsem, o_rsem,
):
    rep = lax.axis_index("rep")
    p = lax.axis_index("patch")
    c = lax.axis_index("grp")
    hpg = heads // GROUPS
    width = hpg * head_dim
    per_group = n_patch // GROUPS
    n_chunk = per_group // 2
    chunk = n_patch // n_chunk
    per_core = chunk // 2
    my_hg = p // per_group
    my_s = p % 2
    my_qc = (p % per_group) // 2

    barrier = pltpu.get_barrier_semaphore()
    n_dev = 2 * n_patch

    def greet(i, carry):
        other = lax.rem(p * 2 + c + i, n_dev)
        pl.semaphore_signal(
            barrier, inc=1, device_id=(rep, other // 2, other % 2), device_id_type=MESH
        )
        return carry

    lax.fori_loop(1, n_dev, greet, 0)
    pl.semaphore_wait(barrier, n_dev - 1)

    pending = []

    def send(src, dst, ssem, rsem, dp, dc):
        away = jnp.logical_or(dp != p, dc != c)
        remote = pltpu.make_async_remote_copy(
            src_ref=src, dst_ref=dst, send_sem=ssem, recv_sem=rsem,
            device_id=(rep, dp, dc), device_id_type=MESH,
        )

        @pl.when(away)
        def _():
            remote.start()

        @pl.when(jnp.logical_not(away))
        def _():
            pltpu.make_async_copy(src, dst, rsem).start()

        pending.append((away, remote))

    def row_slice(i):
        return pl.ds(pl.multiple_of(i * rows, 16), rows)

    def col_slice(g):
        return pl.ds(pl.multiple_of(g * width, 128), width)

    def send_kv(kind, ref):
        stale = kind < 2
        s = (1 - c) if stale else c
        for step in range(GROUPS):
            g = lax.rem(my_hg + 1 + step, GROUPS)
            for qc in range(n_chunk):
                dp = g * per_group + qc * 2 + s
                send(
                    ref.at[:, col_slice(g)], kv.at[kind, row_slice(p), :],
                    kv_ssem.at[kind, step * n_chunk + qc], kv_rsem.at[kind, p], dp, p % 2,
                )

    def prepare(ref, which, dst):
        a = tab_ref[2 * which]
        b = tab_ref[2 * which + 1]
        for h in range(heads):
            cols = slice(h * head_dim, (h + 1) * head_dim)
            xb = ref[:, cols]
            x = xb.astype(jnp.float32)
            xs = jnp.dot(xb, perm_ref[...], preferred_element_type=jnp.float32)
            mean_sq = jnp.mean(x * x, axis=-1, keepdims=True)
            dst[:, cols] = ((x * a + xs * b) * lax.rsqrt(mean_sq + 1e-06)).astype(jnp.bfloat16)

    send_kv(0, sk_ref)
    send_kv(1, sv_ref)
    prepare(q_ref, 0, qrot)
    for step in range(GROUPS):
        g = lax.rem(my_hg + 1 + step, GROUPS)
        dp = g * per_group + (p // chunk) * 2 + c
        dc = (p % chunk) // per_core
        slot = p % per_core
        send(
            qrot.at[:, col_slice(g)], qbuf.at[row_slice(slot), :],
            q_ssem.at[step], q_rsem.at[slot], dp, dc,
        )
    prepare(k_ref, 1, krot)
    send_kv(2, krot)
    send_kv(3, v_ref)

    def kv_wait(kind, src):
        piece = kv.at[kind, row_slice(src), :]
        pltpu.make_async_copy(piece, piece, kv_rsem.at[kind, src]).wait()

    def forward(kind, i):
        src = 2 * i + c
        kv_wait(kind, src)
        piece = kv.at[kind, row_slice(src), :]
        copy = pltpu.make_async_remote_copy(
            src_ref=piece, dst_ref=piece,
            send_sem=f_ssem.at[kind, i], recv_sem=kv_rsem.at[kind, src],
            device_id=(rep, p, 1 - c), device_id_type=MESH,
        )
        copy.start()
        return copy

    forwards = []
    n_q = per_core * rows
    state = [None] * hpg
    inv_root = 1.0 / head_dim**0.5
    blk = chunk * rows
    for part in range(2):
        for i in range(n_patch // 2):
            forwards.append(forward(2 * part, i))
            forwards.append(forward(2 * part + 1, i))
        if part == 0:
            for slot in range(per_core):
                piece = qbuf.at[row_slice(slot), :]
                pltpu.make_async_copy(piece, piece, q_rsem.at[slot]).wait()
        for i in range(n_patch // 2):
            kv_wait(2 * part, 2 * i + (1 - c))
            kv_wait(2 * part + 1, 2 * i + (1 - c))
        side = (1 - my_s) if part == 0 else my_s
        for at in range(0, n_patch * rows, blk):
            bias = bias_ref[pl.ds(side, 1), at : at + blk]
            for h in range(hpg):
                cols = slice(h * head_dim, (h + 1) * head_dim)
                scores = lax.dot_general(
                    qbuf[:, cols], kv[2 * part, at : at + blk, cols],
                    (((1,), (1,)), ((), ())), preferred_element_type=jnp.float32,
                )
                scores = scores * inv_root + bias
                top = jnp.max(scores, axis=1, keepdims=True)
                if state[h] is not None:
                    top = jnp.maximum(top, state[h][0])
                probs = jnp.exp(scores - top)
                total = jnp.sum(probs, axis=1, keepdims=True)
                acc = jnp.dot(
                    probs.astype(jnp.bfloat16), kv[2 * part + 1, at : at + blk, cols],
                    preferred_element_type=jnp.float32,
                )
                if state[h] is not None:
                    fade = jnp.exp(state[h][0] - top)
                    total = total + state[h][1] * fade
                    acc = acc + state[h][2] * fade
                state[h] = (top, total, acc)
    for h in range(hpg):
        cols = slice(h * head_dim, (h + 1) * head_dim)
        osend[:, cols] = (state[h][2] / state[h][1]).astype(jnp.bfloat16)
    for slot in range(per_core):
        dp = my_qc * chunk + c * per_core + slot
        send(
            osend.at[row_slice(slot), :], obuf.at[my_hg],
            o_ssem.at[slot], o_rsem.at[my_hg], dp, my_s,
        )
    for g in range(GROUPS):
        piece = obuf.at[g]
        pltpu.make_async_copy(piece, piece, o_rsem.at[g]).wait()
        out_ref[:, g * width : (g + 1) * width] = obuf[g]
    for copy in forwards:
        copy.wait_send()
    for away, remote in pending:

        @pl.when(away)
        def _():
            remote.wait_send()


def body(n_patch, queries, keys, values, stale_keys, stale_values, q_gain, k_gain, o_weight, slot_positions):
    rows = queries.shape[0]
    head_dim = q_gain.shape[0]
    heads = queries.shape[1] // head_dim
    seq_len = slot_positions.shape[0]
    live_count = seq_len - max(seq_len // 256, 2)
    my_block = lax.axis_index("patch") * 2 + lax.axis_index("grp")
    own_pos = lax.dynamic_slice_in_dim(slot_positions, my_block * rows, rows)
    cosine, sine = tables(own_pos, head_dim)
    order = swap_lanes(head_dim)
    tab = jnp.stack(
        [cosine * q_gain, sine * q_gain[order], cosine * k_gain, sine * k_gain[order]]
    )
    perm = np.zeros((head_dim, head_dim), np.float32)
    perm[order, np.arange(head_dim)] = 1.0
    perm = jnp.asarray(perm, jnp.bfloat16)
    bias = jnp.where(slot_positions < live_count, 0.0, -1e30).astype(jnp.float32)
    bias = bias.reshape(n_patch, 2, rows).transpose(1, 0, 2).reshape(2, n_patch * rows)
    width = heads // GROUPS * head_dim
    n_chunk = n_patch // GROUPS // 2
    per_core = n_patch // n_chunk // 2
    vmem = pl.BlockSpec(memory_space=pltpu.VMEM)
    attn = pl.pallas_call(
        functools.partial(kernel, n_patch, heads, head_dim, rows),
        out_shape=jax.ShapeDtypeStruct(queries.shape, jnp.bfloat16),
        in_specs=[vmem] * 8,
        out_specs=vmem,
        scratch_shapes=[
            pltpu.VMEM(queries.shape, jnp.bfloat16),
            pltpu.VMEM(queries.shape, jnp.bfloat16),
            pltpu.VMEM((per_core * rows, width), jnp.bfloat16),
            pltpu.VMEM((4, n_patch * rows, width), jnp.bfloat16),
            pltpu.VMEM((per_core * rows, width), jnp.bfloat16),
            pltpu.VMEM((GROUPS, rows, width), jnp.bfloat16),
            pltpu.SemaphoreType.DMA((GROUPS,)),
            pltpu.SemaphoreType.DMA((4, GROUPS * n_chunk)),
            pltpu.SemaphoreType.DMA((4, n_patch // 2)),
            pltpu.SemaphoreType.DMA((per_core,)),
            pltpu.SemaphoreType.DMA((per_core,)),
            pltpu.SemaphoreType.DMA((4, n_patch)),
            pltpu.SemaphoreType.DMA((GROUPS,)),
        ],
        compiler_params=pltpu.CompilerParams(
            collective_id=0, has_side_effects=True, vmem_limit_bytes=40 * 1024 * 1024
        ),
    )(queries, keys, values, stale_keys, stale_values, tab, perm, bias)
    projected = jnp.dot(attn, o_weight, preferred_element_type=jnp.float32)
    own_live = own_pos < live_count
    return jnp.where(own_live[:, None], projected, 0.0).astype(jnp.bfloat16)


def solution(mesh):
    split = P(("rep", "patch", "grp"), None)
    in_specs = (split, split, split, split, split, P(), P(), P(), P("rep"))
    return jax.shard_map(
        functools.partial(body, mesh.shape["patch"]),
        mesh=mesh, in_specs=in_specs, out_specs=split, check_vma=False,
    )
```

time: 201 us -> 61.1 us (0.30); the launches traced: 197 us -> 60.6 us
  waiting for transfers between devices: 117 us -> 0 us
  Pallas kernels: 0 us -> 42.4 us
  local copies, waits for them, and re-layouts: 50.8 us -> 8.81 us
  between operations: 13.8 us -> 0.05 us
  matrix products: 9.73 us -> 6.21 us
  other arithmetic: 5.57 us -> 3.17 us
    all_gather x2 -> x0, waiting for transfers between devices: 115 us -> none  [the longest x1 58.3 us: body(): lax.all_gather(partner, 'patch', axis=1, tiled=True)]
    pallas_call x0 -> x1, Pallas kernels: none -> 42.4 us  [body(): pl.pallas_call(functools.partial(kernel, n_patch, heads, head_dim, rows),...]
    slice x4 -> x0, local copies, waits for them, and re-layouts: 19.4 us -> none  [the longest x2 13.4 us: attend(): key_rows = portion[0].reshape(count, head_count, head_dim)]
    unnamed x28 -> x12, local copies, waits for them, and re-layouts: 17.3 us -> 5.47 us
    dot_general x4 -> x0, matrix products: 7.14 us -> none  [the longest x2 4.86 us: attend(): jnp.einsum('qhd,khd->hqk', q_rot, key_rows, preferred_element_type=jnp.fl...]
    gather x2, local copies, waits for them, and re-layouts: 7.72 us -> 3.17 us  [the longest x1 1.59 us: body(): q_gain[order]]
    dot_general x1, matrix products: 2.6 us -> 6.21 us  [body(): projected = jnp.dot(attn, o_weight, preferred_element_type=jnp.float32)]
    another operation x5 -> x1, other arithmetic: 2.49 us -> 0.01 us  [body(): jnp.stack([cosine * q_gain, sine * q_gain[order], cosine * k_gain, sine *...]
  transfers between devices with their start and end apart: 3 -> 0, of which waited for: 3 -> 0; matrix products, arithmetic and copies ran while one was open for 12% -> 0% of each run, Pallas kernels for 0% -> 0%
where the time goes in v1:
time: 61.1 us; the launch traced here: 60.6 us
  Pallas kernels  42.4 us (69%)
  local copies, waits for them, and re-layouts  8.81 us (14%)
  matrix products  6.21 us (10%)
  other arithmetic  3.17 us (5%)
    pallas_call x1, Pallas kernels, body(): pl.pallas_call(functools.partial(kernel, n_patch, heads, head_dim, rows),...  42.4 us
    dot_general x1, matrix products, body(): projected = jnp.dot(attn, o_weight, preferred_element_type=jnp.float32)  6.21 us
    unnamed x12, local copies, waits for them, and re-layouts  5.47 us
    gather x1, local copies, waits for them, and re-layouts, body(): q_gain[order]  1.59 us
    gather x1, local copies, waits for them, and re-layouts, body(): k_gain[order]  1.58 us

profile of v1, /device:TPU:14, one launch (start us, length us, event | category | flops | bytes accessed | tf_op | source)
XLA Modules:
  0.0 60.6 jit_solution(1616043129054355711)
XLA Ops:
  0.0 0.8 %broadcast_compare_fusion = (pred[80]{0:T(512)(128)(4,1)S(1)}, s32[80]{0:T(128)S(1)}) fusion(s32[1280]{0:T(1024)} %param.25, s32[]{:T(128)S(6)} %select_n.82), kind=kLoop, calls=%fused_computation.21 | loop fusion | flops 80 | bytes 724 | tf_op jit(solution)/shard_map/lt | solution.py:270
  0.8 0.7 %pad_clamp_fusion = s32[1024]{0:T(1024)S(1)} fusion(s32[128]{0:T(128)} %constant.87), kind=kLoop, calls=%fused_computation.13 | loop fusion | flops 1024 | bytes 4608 | tf_op jit(solution)/shard_map/gather | solution.py:234
  1.5 1.6 %gather_fusion.1 = f32[128]{0:T(128)S(1)} fusion(f32[128]{0:T(128)} %param.23, s32[1024]{0:T(1024)S(1)} %pad_clamp_fusion), kind=kCustom, calls=%fused_computation.1 | custom fusion | bytes 1536 | tf_op jit(solution)/shard_map/gather | solution.py:234
  3.0 1.6 %gather_fusion = f32[128]{0:T(128)S(1)} fusion(f32[128]{0:T(128)} %param.22, s32[1024]{0:T(1024)S(1)} %pad_clamp_fusion), kind=kCustom, calls=%fused_computation | custom fusion | bytes 1536 | tf_op jit(solution)/shard_map/gather | solution.py:234
  4.6 0.7 %compare_select_fusion = f32[1280]{0:T(1024)S(1)} fusion(s32[1280]{0:T(1024)} %param.25), kind=kLoop, calls=%fused_computation.12 | loop fusion | flops 2560 | bytes 10240 | tf_op jit(solution)/shard_map/jit(_where)/select_n | solution.py:239
  5.3 0.1 reshape.639
  5.4 0.1 reshape.640.bias_ref
  5.5 1.0 %fusion.5 = (f32[1,80,128]{2,1,0:T(8,128)S(1)}, f32[1,80,128]{2,1,0:T(8,128)S(1)}, f32[1,80,128]{2,1,0:T(8,128)S(1)}, f32[1,80,128]{2,1,0:T(8,128)S(1)}) fusion(f32[128]{0:T(128)S(1)} %gather_fusion, f32[128]{0:T(128)} %constant.73.clone, f32[128]{0:T(128)} %constant.72.clone, f32[80]{0:T(128)S(1)} %get-tuple-element.13, f32[80]{0:T(128)S(1)} %get-tuple-element.12, ...), kind=kLoop, calls=%fused_computation.11 | loop fusion | flops 81920 | bytes 168128 | tf_op jit(solution)/shard_map/mul | solution.py:234
  6.5 0.0 copy-start
  6.6 0.9 %copy-done = bf16[80,1536]{1,0:T(8,128)(2,1)S(1)} copy-done((bf16[80,1536]{1,0:T(8,128)(2,1)S(1)}, bf16[80,1536]{1,0:T(8,128)(2,1)}, u32[]{:S(2)}) %copy-start) | copy-done | bytes 245784
  7.5 0.0 copy-start.1
  7.5 0.9 %copy-done.1 = bf16[80,1536]{1,0:T(8,128)(2,1)S(1)} copy-done((bf16[80,1536]{1,0:T(8,128)(2,1)S(1)}, bf16[80,1536]{1,0:T(8,128)(2,1)}, u32[]{:S(2)}) %copy-start.1) | copy-done | bytes 245784
  8.4 0.0 copy-start.2
  8.4 0.9 %copy-done.2 = bf16[80,1536]{1,0:T(8,128)(2,1)S(1)} copy-done((bf16[80,1536]{1,0:T(8,128)(2,1)S(1)}, bf16[80,1536]{1,0:T(8,128)(2,1)}, u32[]{:S(2)}) %copy-start.2) | copy-done | bytes 245784
  9.4 0.0 copy-start.3
  9.4 0.9 %copy-done.3 = bf16[80,1536]{1,0:T(8,128)(2,1)S(1)} copy-done((bf16[80,1536]{1,0:T(8,128)(2,1)S(1)}, bf16[80,1536]{1,0:T(8,128)(2,1)}, u32[]{:S(2)}) %copy-start.3) | copy-done | bytes 245784
  10.3 0.0 copy-start.4
  10.3 0.9 %copy-done.4 = bf16[80,1536]{1,0:T(8,128)(2,1)S(1)} copy-done((bf16[80,1536]{1,0:T(8,128)(2,1)S(1)}, bf16[80,1536]{1,0:T(8,128)(2,1)}, u32[]{:S(2)}) %copy-start.4) | copy-done | bytes 245784
  11.3 0.0 copy-start.5
  11.3 0.8 %copy-done.5 = bf16[128,128]{1,0:T(8,128)(2,1)S(1)} copy-done((bf16[128,128]{1,0:T(8,128)(2,1)S(1)}, bf16[128,128]{1,0:T(8,128)(2,1)}, u32[]{:S(2)}) %copy-start.5) | copy-done | bytes 32792
  12.0 42.4 %shard_map.163 = bf16[80,1536]{1,0:T(8,128)(2,1)S(1)} custom-call(bf16[80,1536]{1,0:T(8,128)(2,1)S(1)} %copy-done, bf16[80,1536]{1,0:T(8,128)(2,1)S(1)} %copy-done.1, bf16[80,1536]{1,0:T(8,128)(2,1)S(1)} %copy-done.2, bf16[80,1536]{1,0:T(8,128)(2,1)S(1)} %copy-done.3, bf16[80,1536]{1,0:T(8,128)(2,1)S(1)} %copy-done.4, ...), custom_call_target="tpu_custom_call" | custom-call | tf_op jit(solution)/shard_map/pallas_call | solution.py:245
  54.4 6.2 %fusion = bf16[80,3072]{1,0:T(8,128)(2,1)} fusion(bf16[80,1536]{1,0:T(8,128)(2,1)S(1)} %shard_map.163, bf16[1536,3072]{1,0:T(8,128)(2,1)} %param.24, pred[80]{0:T(512)(128)(4,1)S(1)} %get-tuple-element.5), kind=kOutput, calls=%fused_computation.3 | convolution fusion | flops 755466240 | bytes 10174544 | tf_op jit(solution)/shard_map/dot_general | solution.py:269
  (3 shorter events, 0.0 us)
Async XLA Ops:
  6.5 0.9 %copy-start = (bf16[80,1536]{1,0:T(8,128)(2,1)S(1)}, bf16[80,1536]{1,0:T(8,128)(2,1)}, u32[]{:S(2)}) copy-start(bf16[80,1536]{1,0:T(8,128)(2,1)} %q_ref.1) | copy-start | bytes 737284
  7.5 0.9 %copy-start.1 = (bf16[80,1536]{1,0:T(8,128)(2,1)S(1)}, bf16[80,1536]{1,0:T(8,128)(2,1)}, u32[]{:S(2)}) copy-start(bf16[80,1536]{1,0:T(8,128)(2,1)} %k_ref.1) | copy-start | bytes 737284
  8.4 0.9 %copy-start.2 = (bf16[80,1536]{1,0:T(8,128)(2,1)S(1)}, bf16[80,1536]{1,0:T(8,128)(2,1)}, u32[]{:S(2)}) copy-start(bf16[80,1536]{1,0:T(8,128)(2,1)} %v_ref.1) | copy-start | bytes 737284
  9.4 0.9 %copy-start.3 = (bf16[80,1536]{1,0:T(8,128)(2,1)S(1)}, bf16[80,1536]{1,0:T(8,128)(2,1)}, u32[]{:S(2)}) copy-start(bf16[80,1536]{1,0:T(8,128)(2,1)} %sk_ref.1) | copy-start | bytes 737284
  10.3 0.9 %copy-start.4 = (bf16[80,1536]{1,0:T(8,128)(2,1)S(1)}, bf16[80,1536]{1,0:T(8,128)(2,1)}, u32[]{:S(2)}) copy-start(bf16[80,1536]{1,0:T(8,128)(2,1)} %sv_ref.1) | copy-start | bytes 737284
  11.3 0.8 %copy-start.5 = (bf16[128,128]{1,0:T(8,128)(2,1)S(1)}, bf16[128,128]{1,0:T(8,128)(2,1)}, u32[]{:S(2)}) copy-start(bf16[128,128]{1,0:T(8,128)(2,1)} %constant.78.clone.perm_ref) | copy-start | bytes 98308

commit v2 on v1

--- a/solution.py
+++ b/solution.py
@@ -1,8 +1,8 @@
 import functools
+import math
 
 import jax
 import jax.numpy as jnp
-import numpy as np
 from jax import lax
 from jax.experimental import pallas as pl
 from jax.experimental.pallas import tpu as pltpu
@@ -14,43 +14,60 @@
 MESH = pl.DeviceIdType.MESH
 
 
-def swap_lanes(head_dim):
-    order = []
+def sections(head_dim):
+    return (head_dim // 8, 7 * head_dim // 16, 7 * head_dim // 16)
+
+
+def by_lane(lanes, head_dim, values):
+    out = values[-1][2]
+    for _, end, value in reversed(values[:-1]):
+        out = jnp.where(lanes < end, value, out)
+    return out
+
+
+def rotary_tables(pos, head_dim):
+    lanes = lax.broadcasted_iota(jnp.int32, (1, head_dim), 1)
+    wide = lax.broadcasted_iota(jnp.int32, (head_dim, head_dim), 1)
+    down = lax.broadcasted_iota(jnp.int32, (head_dim, head_dim), 0)
+    line = jnp.floor((pos + 0.5) * (1.0 / LAT_W))
+    col = pos - line * LAT_W
+    frame = jnp.floor((line + 0.5) * (1.0 / LAT_H))
+    row = line - frame * LAT_H
     at = 0
-    for width in (head_dim // 8, 7 * head_dim // 16, 7 * head_dim // 16):
+    starts, scales, signs, shifts, coords = [], [], [], [], []
+    for width, coord in zip(sections(head_dim), (frame, row, col)):
         half = width // 2
-        order += list(range(at + half, at + width)) + list(range(at, at + half))
+        rate = -2.0 / width * math.log(256.0)
+        for k in range(2):
+            lo, hi = at + k * half, at + (k + 1) * half
+            starts.append((lo, hi, float(lo)))
+            scales.append((lo, hi, rate))
+            signs.append((lo, hi, 1.0 if k else -1.0))
+            shifts.append((lo, hi, -half if k else half))
+        coords.append((at, at + width, coord))
         at += width
-    return np.array(order)
-
-
-def tables(pos_ids, head_dim):
-    per_frame = LAT_H * LAT_W
-    coords = (pos_ids // per_frame, pos_ids // LAT_W % LAT_H, pos_ids % LAT_W)
-    freq = []
-    which = []
-    sign = []
-    for idx, width in enumerate((head_dim // 8, 7 * head_dim // 16, 7 * head_dim // 16)):
-        half = width // 2
-        f = np.float32(256.0) ** (-np.arange(half, dtype=np.float32) * np.float32(2.0) / np.float32(width))
-        freq += list(f) + list(f)
-        which += [idx] * width
-        sign += [-1.0] * half + [1.0] * half
-    freq = jnp.asarray(np.array(freq, np.float32))[None, :]
-    which = np.array(which)[None, :]
-    sign = jnp.asarray(np.array(sign, np.float32))[None, :]
-    f_pos, r_pos, c_pos = (x.astype(jnp.float32)[:, None] for x in coords)
-    coord = jnp.where(which == 0, f_pos, jnp.where(which == 1, r_pos, c_pos))
-    angles = coord * freq
-    return jnp.cos(angles), jnp.sin(angles) * sign
+    step = lanes.astype(jnp.float32) - by_lane(lanes, head_dim, starts)
+    freq = jnp.exp(step * by_lane(lanes, head_dim, scales))
+    angles = by_lane(lanes, head_dim, coords) * freq
+    swap = (down == wide + by_lane(wide, head_dim, shifts)).astype(jnp.float32)
+    return jnp.cos(angles), jnp.sin(angles) * by_lane(lanes, head_dim, signs), swap
+
+
+def row_to_column(row):
+    n = row.shape[1]
+    same = lax.broadcasted_iota(jnp.int32, (n, n), 0) == lax.broadcasted_iota(
+        jnp.int32, (n, n), 1
+    )
+    return jnp.sum(jnp.where(same, row, 0.0), axis=1, keepdims=True)
 
 
 def kernel(
     n_patch, heads, head_dim, rows,
-    q_ref, k_ref, v_ref, sk_ref, sv_ref, tab_ref, perm_ref, bias_ref,
+    q_hbm, k_hbm, v_ref, sk_ref, sv_ref, qg_hbm, kg_hbm, w_hbm, pos_hbm,
     out_ref,
+    q_ref, k_ref, qg_ref, kg_ref, w_ref, pos_ref,
     qrot, krot, qbuf, kv, osend, obuf,
-    q_ssem, kv_ssem, f_ssem, o_ssem, q_rsem, kv_rsem, o_rsem,
+    l_sem, q_ssem, kv_ssem, f_ssem, o_ssem, q_rsem, kv_rsem, o_rsem,
 ):
     rep = lax.axis_index("rep")
     p = lax.axis_index("patch")
@@ -65,6 +82,21 @@
     my_s = p % 2
     my_qc = (p % per_group) // 2
 
+    seq_len = 2 * n_patch * rows
+    live_count = float(seq_len - max(seq_len // 256, 2))
+
+    loads = [
+        pltpu.make_async_copy(src, dst, l_sem.at[i])
+        for i, (src, dst) in enumerate(
+            (
+                (pos_hbm, pos_ref), (qg_hbm, qg_ref), (kg_hbm, kg_ref),
+                (q_hbm, q_ref), (k_hbm, k_ref), (w_hbm, w_ref),
+            )
+        )
+    ]
+    for load in loads[:5]:
+        load.start()
+
     barrier = pltpu.get_barrier_semaphore()
     n_dev = 2 * n_patch
 
@@ -115,20 +147,27 @@
                     kv_ssem.at[kind, step * n_chunk + qc], kv_rsem.at[kind, p], dp, p % 2,
                 )
 
-    def prepare(ref, which, dst):
-        a = tab_ref[2 * which]
-        b = tab_ref[2 * which + 1]
+    def prepare(ref, gain_ref, dst):
+        gain = gain_ref[...]
+        a = cosine * gain
+        b = sine * jnp.sum(swap * row_to_column(gain), axis=0, keepdims=True)
         for h in range(heads):
             cols = slice(h * head_dim, (h + 1) * head_dim)
             xb = ref[:, cols]
             x = xb.astype(jnp.float32)
-            xs = jnp.dot(xb, perm_ref[...], preferred_element_type=jnp.float32)
+            xs = jnp.dot(xb, swap_b, preferred_element_type=jnp.float32)
             mean_sq = jnp.mean(x * x, axis=-1, keepdims=True)
             dst[:, cols] = ((x * a + xs * b) * lax.rsqrt(mean_sq + 1e-06)).astype(jnp.bfloat16)
 
     send_kv(0, sk_ref)
     send_kv(1, sv_ref)
-    prepare(q_ref, 0, qrot)
+    loads[5].start()
+    for load in loads[:5]:
+        load.wait()
+    pos = row_to_column(pos_ref[pl.ds(p * 2 + c, 1), :].astype(jnp.float32))
+    cosine, sine, swap = rotary_tables(pos, head_dim)
+    swap_b = swap.astype(jnp.bfloat16)
+    prepare(q_ref, qg_ref, qrot)
     for step in range(GROUPS):
         g = lax.rem(my_hg + 1 + step, GROUPS)
         dp = g * per_group + (p // chunk) * 2 + c
@@ -138,7 +177,7 @@
             qrot.at[:, col_slice(g)], qbuf.at[row_slice(slot), :],
             q_ssem.at[step], q_rsem.at[slot], dp, dc,
         )
-    prepare(k_ref, 1, krot)
+    prepare(k_ref, kg_ref, krot)
     send_kv(2, krot)
     send_kv(3, v_ref)
 
@@ -176,7 +215,11 @@
             kv_wait(2 * part + 1, 2 * i + (1 - c))
         side = (1 - my_s) if part == 0 else my_s
         for at in range(0, n_patch * rows, blk):
-            bias = bias_ref[pl.ds(side, 1), at : at + blk]
+            first = at // rows
+            key_pos = jnp.concatenate(
+                [pos_ref[pl.ds(2 * i + side, 1), :] for i in range(first, first + chunk)], axis=1
+            )
+            bias = jnp.where(key_pos.astype(jnp.float32) < live_count, 0.0, -1e30)
             for h in range(hpg):
                 cols = slice(h * head_dim, (h + 1) * head_dim)
                 scores = lax.dot_general(
@@ -210,7 +253,13 @@
     for g in range(GROUPS):
         piece = obuf.at[g]
         pltpu.make_async_copy(piece, piece, o_rsem.at[g]).wait()
-        out_ref[:, g * width : (g + 1) * width] = obuf[g]
+    attn = jnp.concatenate([obuf[g] for g in range(GROUPS)], axis=1)
+    loads[5].wait()
+    own_live = pos < live_count
+    d_out = out_ref.shape[1]
+    for at in range(0, d_out, 512):
+        tile = jnp.dot(attn, w_ref[:, at : at + 512], preferred_element_type=jnp.float32)
+        out_ref[:, at : at + 512] = jnp.where(own_live, tile, 0.0).astype(jnp.bfloat16)
     for copy in forwards:
         copy.wait_send()
     for away, remote in pending:
@@ -224,36 +273,29 @@
     rows = queries.shape[0]
     head_dim = q_gain.shape[0]
     heads = queries.shape[1] // head_dim
-    seq_len = slot_positions.shape[0]
-    live_count = seq_len - max(seq_len // 256, 2)
-    my_block = lax.axis_index("patch") * 2 + lax.axis_index("grp")
-    own_pos = lax.dynamic_slice_in_dim(slot_positions, my_block * rows, rows)
-    cosine, sine = tables(own_pos, head_dim)
-    order = swap_lanes(head_dim)
-    tab = jnp.stack(
-        [cosine * q_gain, sine * q_gain[order], cosine * k_gain, sine * k_gain[order]]
-    )
-    perm = np.zeros((head_dim, head_dim), np.float32)
-    perm[order, np.arange(head_dim)] = 1.0
-    perm = jnp.asarray(perm, jnp.bfloat16)
-    bias = jnp.where(slot_positions < live_count, 0.0, -1e30).astype(jnp.float32)
-    bias = bias.reshape(n_patch, 2, rows).transpose(1, 0, 2).reshape(2, n_patch * rows)
     width = heads // GROUPS * head_dim
     n_chunk = n_patch // GROUPS // 2
     per_core = n_patch // n_chunk // 2
-    vmem = pl.BlockSpec(memory_space=pltpu.VMEM)
-    attn = pl.pallas_call(
+    hbm = pl.BlockSpec(memory_space=pl.ANY)
+    return pl.pallas_call(
         functools.partial(kernel, n_patch, heads, head_dim, rows),
-        out_shape=jax.ShapeDtypeStruct(queries.shape, jnp.bfloat16),
-        in_specs=[vmem] * 8,
-        out_specs=vmem,
+        out_shape=jax.ShapeDtypeStruct((rows, o_weight.shape[1]), jnp.bfloat16),
+        in_specs=[hbm] * 9,
+        out_specs=pl.BlockSpec(memory_space=pltpu.VMEM),
         scratch_shapes=[
+            pltpu.VMEM(queries.shape, jnp.bfloat16),
+            pltpu.VMEM(queries.shape, jnp.bfloat16),
+            pltpu.VMEM((1, head_dim), jnp.float32),
+            pltpu.VMEM((1, head_dim), jnp.float32),
+            pltpu.VMEM(o_weight.shape, jnp.bfloat16),
+            pltpu.VMEM((2 * n_patch, rows), jnp.int32),
             pltpu.VMEM(queries.shape, jnp.bfloat16),
             pltpu.VMEM(queries.shape, jnp.bfloat16),
             pltpu.VMEM((per_core * rows, width), jnp.bfloat16),
             pltpu.VMEM((4, n_patch * rows, width), jnp.bfloat16),
             pltpu.VMEM((per_core * rows, width), jnp.bfloat16),
             pltpu.VMEM((GROUPS, rows, width), jnp.bfloat16),
+            pltpu.SemaphoreType.DMA((6,)),
             pltpu.SemaphoreType.DMA((GROUPS,)),
             pltpu.SemaphoreType.DMA((4, GROUPS * n_chunk)),
             pltpu.SemaphoreType.DMA((4, n_patch // 2)),
@@ -265,10 +307,11 @@
         compiler_params=pltpu.CompilerParams(
             collective_id=0, has_side_effects=True, vmem_limit_bytes=40 * 1024 * 1024
         ),
-    )(queries, keys, values, stale_keys, stale_values, tab, perm, bias)
-    projected = jnp.dot(attn, o_weight, preferred_element_type=jnp.float32)
-    own_live = own_pos < live_count
-    return jnp.where(own_live[:, None], projected, 0.0).astype(jnp.bfloat16)
+    )(
+        queries, keys, values, stale_keys, stale_values,
+        q_gain.reshape(1, head_dim), k_gain.reshape(1, head_dim), o_weight,
+        slot_positions.reshape(2 * n_patch, rows),
+    )
 
 
 def solution(mesh):

time: 61.1 us -> 56.6 us (0.926)
  matrix products: 6.21 us -> 0 us
  other arithmetic: 3.17 us -> 0 us
  Pallas kernels: 42.4 us -> 44.9 us
  local copies, waits for them, and re-layouts: 8.81 us -> 11.3 us
    dot_general x1 -> x0, matrix products: 6.21 us -> none  [body(): projected = jnp.dot(attn, o_weight, preferred_element_type=jnp.float32)]
    unnamed x12 -> x17, local copies, waits for them, and re-layouts: 5.47 us -> 10.5 us
    gather x2 -> x0, local copies, waits for them, and re-layouts: 3.17 us -> none  [the longest x1 1.59 us: body(): q_gain[order]]
    pallas_call x1, Pallas kernels: 42.4 us -> 44.9 us  [body(): pl.pallas_call(functools.partial(kernel, n_patch, heads, head_dim, rows),...]
    mul x1 -> x0, other arithmetic: 0.99 us -> none  [body(): sine * q_gain[order]]
    lt x1 -> x0, other arithmetic: 0.77 us -> none  [body(): own_live = own_pos < live_count]
    select_n x1 -> x0, other arithmetic: 0.71 us -> none  [body(): jnp.where(slot_positions < live_count, 0.0, -1e+30).astype(jnp.float32)]
    gather x1 -> x0, other arithmetic: 0.66 us -> none  [body(): q_gain[order]]
where the time goes in v2:
time: 56.6 us; the launch traced here: 56.2 us
  Pallas kernels  44.9 us (79%)
  local copies, waits for them, and re-layouts  11.3 us (20%)
    pallas_call x1, Pallas kernels, body(): pl.pallas_call(functools.partial(kernel, n_patch, heads, head_dim, rows),...  44.9 us
    unnamed x17, local copies, waits for them, and re-layouts  10.5 us

profile of v2, /device:TPU:14, one launch (start us, length us, event | category | flops | bytes accessed | tf_op | source)
XLA Modules:
  0.0 56.2 jit_solution(13918821738768610829)
XLA Ops:
  0.0 0.8 %reshape.11.pos_hbm = s32[16,80]{1,0:T(8,128)S(1)} reshape(s32[1280]{0:T(1024)} %param.17) | data formatting | bytes 10240 | tf_op jit(solution)/shard_map/reshape | solution.py:313
  0.8 0.0 copy-start
  0.8 3.7 %copy-done = bf16[1536,3072]{1,0:T(8,128)(2,1)S(1)} copy-done((bf16[1536,3072]{1,0:T(8,128)(2,1)S(1)}, bf16[1536,3072]{1,0:T(8,128)(2,1)}, u32[]{:S(2)}) %copy-start) | copy-done | bytes 9437208
  4.5 0.0 copy-start.1
  4.5 0.9 %copy-done.1 = bf16[80,1536]{1,0:T(8,128)(2,1)S(1)} copy-done((bf16[80,1536]{1,0:T(8,128)(2,1)S(1)}, bf16[80,1536]{1,0:T(8,128)(2,1)}, u32[]{:S(2)}) %copy-start.1) | copy-done | bytes 245784
  5.4 0.0 copy-start.2
  5.4 0.9 %copy-done.2 = bf16[80,1536]{1,0:T(8,128)(2,1)S(1)} copy-done((bf16[80,1536]{1,0:T(8,128)(2,1)S(1)}, bf16[80,1536]{1,0:T(8,128)(2,1)}, u32[]{:S(2)}) %copy-start.2) | copy-done | bytes 245784
  6.3 0.0 copy-start.3
  6.3 0.9 %copy-done.3 = bf16[80,1536]{1,0:T(8,128)(2,1)S(1)} copy-done((bf16[80,1536]{1,0:T(8,128)(2,1)S(1)}, bf16[80,1536]{1,0:T(8,128)(2,1)}, u32[]{:S(2)}) %copy-start.3) | copy-done | bytes 245784
  7.3 0.0 copy-start.4
  7.3 0.9 %copy-done.4 = bf16[80,1536]{1,0:T(8,128)(2,1)S(1)} copy-done((bf16[80,1536]{1,0:T(8,128)(2,1)S(1)}, bf16[80,1536]{1,0:T(8,128)(2,1)}, u32[]{:S(2)}) %copy-start.4) | copy-done | bytes 245784
  8.2 0.0 copy-start.5
  8.2 0.9 %copy-done.5 = bf16[80,1536]{1,0:T(8,128)(2,1)S(1)} copy-done((bf16[80,1536]{1,0:T(8,128)(2,1)S(1)}, bf16[80,1536]{1,0:T(8,128)(2,1)}, u32[]{:S(2)}) %copy-start.5) | copy-done | bytes 245784
  9.2 0.0 copy-start.6
  9.2 0.7 %copy-done.6 = f32[128]{0:T(128)S(1)} copy-done((f32[128]{0:T(128)S(1)}, f32[128]{0:T(128)}, u32[]{:S(2)}) %copy-start.6) | copy-done | bytes 536
  9.8 0.0 copy-start.7
  9.8 0.7 %copy-done.7 = f32[128]{0:T(128)S(1)} copy-done((f32[128]{0:T(128)S(1)}, f32[128]{0:T(128)}, u32[]{:S(2)}) %copy-start.7) | copy-done | bytes 536
  10.5 44.9 %shard_map.91 = bf16[80,3072]{1,0:T(8,128)(2,1)S(1)} custom-call(bf16[80,1536]{1,0:T(8,128)(2,1)S(1)} %copy-done.1, bf16[80,1536]{1,0:T(8,128)(2,1)S(1)} %copy-done.2, bf16[80,1536]{1,0:T(8,128)(2,1)S(1)} %copy-done.3, bf16[80,1536]{1,0:T(8,128)(2,1)S(1)} %copy-done.4, bf16[80,1536]{1,0:T(8,128)(2,1)S(1)} %copy-done.5, f32[1,128]{1,0:T(1,128)S(1)} %bitcast.2, ...), custom_call_target="tpu_custom_call" | custom-call | tf_op jit(solution)/shard_map/pallas_call | solution.py:280
  55.4 0.8 %copy.11 = bf16[80,3072]{1,0:T(8,128)(2,1)} copy(bf16[80,3072]{1,0:T(8,128)(2,1)S(1)} %shard_map.91) | data formatting | bytes 983040
Async XLA Ops:
  0.8 3.7 %copy-start = (bf16[1536,3072]{1,0:T(8,128)(2,1)S(1)}, bf16[1536,3072]{1,0:T(8,128)(2,1)}, u32[]{:S(2)}) copy-start(bf16[1536,3072]{1,0:T(8,128)(2,1)} %w_hbm.1) | copy-start | bytes 28311556
  4.5 0.9 %copy-start.1 = (bf16[80,1536]{1,0:T(8,128)(2,1)S(1)}, bf16[80,1536]{1,0:T(8,128)(2,1)}, u32[]{:S(2)}) copy-start(bf16[80,1536]{1,0:T(8,128)(2,1)} %q_hbm.1) | copy-start | bytes 737284
  5.4 0.9 %copy-start.2 = (bf16[80,1536]{1,0:T(8,128)(2,1)S(1)}, bf16[80,1536]{1,0:T(8,128)(2,1)}, u32[]{:S(2)}) copy-start(bf16[80,1536]{1,0:T(8,128)(2,1)} %k_hbm.1) | copy-start | bytes 737284
  6.3 0.9 %copy-start.3 = (bf16[80,1536]{1,0:T(8,128)(2,1)S(1)}, bf16[80,1536]{1,0:T(8,128)(2,1)}, u32[]{:S(2)}) copy-start(bf16[80,1536]{1,0:T(8,128)(2,1)} %v_ref.1) | copy-start | bytes 737284
  7.3 0.9 %copy-start.4 = (bf16[80,1536]{1,0:T(8,128)(2,1)S(1)}, bf16[80,1536]{1,0:T(8,128)(2,1)}, u32[]{:S(2)}) copy-start(bf16[80,1536]{1,0:T(8,128)(2,1)} %sk_ref.1) | copy-start | bytes 737284
  8.2 0.9 %copy-start.5 = (bf16[80,1536]{1,0:T(8,128)(2,1)S(1)}, bf16[80,1536]{1,0:T(8,128)(2,1)}, u32[]{:S(2)}) copy-start(bf16[80,1536]{1,0:T(8,128)(2,1)} %sv_ref.1) | copy-start | bytes 737284
  9.2 0.7 %copy-start.6 = (f32[128]{0:T(128)S(1)}, f32[128]{0:T(128)}, u32[]{:S(2)}) copy-start(f32[128]{0:T(128)} %param.14) | copy-start | bytes 1540
  9.8 0.7 %copy-start.7 = (f32[128]{0:T(128)S(1)}, f32[128]{0:T(128)}, u32[]{:S(2)}) copy-start(f32[128]{0:T(128)} %param.15) | copy-start | bytes 1540

commit v3 on v2

--- a/solution.py
+++ b/solution.py
@@ -276,7 +276,7 @@
     width = heads // GROUPS * head_dim
     n_chunk = n_patch // GROUPS // 2
     per_core = n_patch // n_chunk // 2
-    hbm = pl.BlockSpec(memory_space=pl.ANY)
+    hbm = pl.BlockSpec(memory_space=pltpu.HBM)
     return pl.pallas_call(
         functools.partial(kernel, n_patch, heads, head_dim, rows),
         out_shape=jax.ShapeDtypeStruct((rows, o_weight.shape[1]), jnp.bfloat16),
@@ -305,7 +305,7 @@
             pltpu.SemaphoreType.DMA((GROUPS,)),
         ],
         compiler_params=pltpu.CompilerParams(
-            collective_id=0, has_side_effects=True, vmem_limit_bytes=40 * 1024 * 1024
+            collective_id=0, has_side_effects=True, vmem_limit_bytes=60 * 1024 * 1024
         ),
     )(
         queries, keys, values, stale_keys, stale_values,

time: 56.6 us -> 48.6 us (0.86)
  local copies, waits for them, and re-layouts: 11.3 us -> 3.21 us
    unnamed x17 -> x1, local copies, waits for them, and re-layouts: 10.5 us -> 1.84 us
    reshape x1, local copies, waits for them, and re-layouts: 0.77 us -> 1.37 us  [body(): slot_positions.reshape(2 * n_patch, rows)]
where the time goes in v3:
time: 48.6 us; the launch traced here: 48.4 us
  Pallas kernels  45.2 us (93%)
  local copies, waits for them, and re-layouts  3.21 us (7%)
    pallas_call x1, Pallas kernels, body(): pl.pallas_call(functools.partial(kernel, n_patch, heads, head_dim, rows),...  45.2 us
    unnamed x1, local copies, waits for them, and re-layouts  1.84 us
    reshape x1, local copies, waits for them, and re-layouts, body(): slot_positions.reshape(2 * n_patch, rows)  1.37 us

profile of v3, /device:TPU:14, one launch (start us, length us, event | category | flops | bytes accessed | tf_op | source)
XLA Modules:
  0.0 48.4 jit_solution(734394057852838074)
XLA Ops:
  0.0 1.4 %reshape.11.pos_hbm = s32[16,80]{1,0:T(8,128)} reshape(s32[1280]{0:T(1024)} %param.17) | data formatting | bytes 10240 | tf_op jit(solution)/shard_map/reshape | solution.py:313
  1.4 45.2 %shard_map.91 = bf16[80,3072]{1,0:T(8,128)(2,1)} custom-call(bf16[80,1536]{1,0:T(8,128)(2,1)} %q_hbm.1, bf16[80,1536]{1,0:T(8,128)(2,1)} %k_hbm.1, bf16[80,1536]{1,0:T(8,128)(2,1)} %v_ref.1, bf16[80,1536]{1,0:T(8,128)(2,1)} %sk_ref.1, bf16[80,1536]{1,0:T(8,128)(2,1)} %sv_ref.1, f32[1,128]{1,0:T(1,128)} %bitcast.2, f32[1,128]{1,0:T(1,128)} %bitcast.3, ...), custom_call_target="tpu_custom_call" | custom-call | tf_op jit(solution)/shard_map/pallas_call | solution.py:280
  46.6 1.8 %copy.11 = bf16[80,3072]{1,0:T(8,128)(2,1)} copy(bf16[80,3072]{1,0:T(8,128)(2,1)} %shard_map.91) | data formatting | bytes 983040

commit v4 on v3

--- a/solution.py
+++ b/solution.py
@@ -164,7 +164,11 @@
     loads[5].start()
     for load in loads[:5]:
         load.wait()
-    pos = row_to_column(pos_ref[pl.ds(p * 2 + c, 1), :].astype(jnp.float32))
+    all_pos = pos_ref[...].reshape(1, seq_len).astype(jnp.float32)
+    here = lax.broadcasted_iota(jnp.int32, (rows, seq_len), 1) == (
+        lax.broadcasted_iota(jnp.int32, (rows, seq_len), 0) + (p * 2 + c) * rows
+    )
+    pos = jnp.sum(jnp.where(here, all_pos, 0.0), axis=1, keepdims=True)
     cosine, sine, swap = rotary_tables(pos, head_dim)
     swap_b = swap.astype(jnp.bfloat16)
     prepare(q_ref, qg_ref, qrot)
@@ -216,10 +220,18 @@
         side = (1 - my_s) if part == 0 else my_s
         for at in range(0, n_patch * rows, blk):
             first = at // rows
-            key_pos = jnp.concatenate(
-                [pos_ref[pl.ds(2 * i + side, 1), :] for i in range(first, first + chunk)], axis=1
+            even, odd = (
+                jnp.concatenate(
+                    [
+                        all_pos[:, (2 * i + k) * rows : (2 * i + k + 1) * rows]
+                        for i in range(first, first + chunk)
+                    ],
+                    axis=1,
+                )
+                for k in range(2)
             )
-            bias = jnp.where(key_pos.astype(jnp.float32) < live_count, 0.0, -1e30)
+            key_pos = jnp.where(side == 0, even, odd)
+            bias = jnp.where(key_pos < live_count, 0.0, -1e30)
             for h in range(hpg):
                 cols = slice(h * head_dim, (h + 1) * head_dim)
                 scores = lax.dot_general(
@@ -288,7 +300,7 @@
             pltpu.VMEM((1, head_dim), jnp.float32),
             pltpu.VMEM((1, head_dim), jnp.float32),
             pltpu.VMEM(o_weight.shape, jnp.bfloat16),
-            pltpu.VMEM((2 * n_patch, rows), jnp.int32),
+            pltpu.VMEM((2 * n_patch * rows,), jnp.int32),
             pltpu.VMEM(queries.shape, jnp.bfloat16),
             pltpu.VMEM(queries.shape, jnp.bfloat16),
             pltpu.VMEM((per_core * rows, width), jnp.bfloat16),
@@ -310,7 +322,7 @@
     )(
         queries, keys, values, stale_keys, stale_values,
         q_gain.reshape(1, head_dim), k_gain.reshape(1, head_dim), o_weight,
-        slot_positions.reshape(2 * n_patch, rows),
+        slot_positions,
     )
 
 

time: 48.6 us -> 47.3 us (0.973)
  local copies, waits for them, and re-layouts: 3.21 us -> 1.84 us
    reshape x1 -> x0, local copies, waits for them, and re-layouts: 1.37 us -> none  [body(): slot_positions.reshape(2 * n_patch, rows)]
where the time goes in v4:
time: 47.3 us; the launch traced here: 47.1 us
  Pallas kernels  45.3 us (96%)
  local copies, waits for them, and re-layouts  1.84 us (4%)
    pallas_call x1, Pallas kernels, body(): pl.pallas_call(functools.partial(kernel, n_patch, heads, head_dim, rows),...  45.3 us
    unnamed x1, local copies, waits for them, and re-layouts  1.84 us

profile of v4, /device:TPU:14, one launch (start us, length us, event | category | flops | bytes accessed | tf_op | source)
XLA Modules:
  0.0 47.1 jit_solution(11305492361889512239)
XLA Ops:
  0.0 45.3 %shard_map.91 = bf16[80,3072]{1,0:T(8,128)(2,1)} custom-call(bf16[80,1536]{1,0:T(8,128)(2,1)} %q_hbm.1, bf16[80,1536]{1,0:T(8,128)(2,1)} %k_hbm.1, bf16[80,1536]{1,0:T(8,128)(2,1)} %v_ref.1, bf16[80,1536]{1,0:T(8,128)(2,1)} %sk_ref.1, bf16[80,1536]{1,0:T(8,128)(2,1)} %sv_ref.1, f32[1,128]{1,0:T(1,128)} %bitcast.2, f32[1,128]{1,0:T(1,128)} %bitcast.3, ...), custom_call_target="tpu_custom_call" | custom-call | tf_op jit(solution)/shard_map/pallas_call | solution.py:292
  45.3 1.8 %copy.11 = bf16[80,3072]{1,0:T(8,128)(2,1)} copy(bf16[80,3072]{1,0:T(8,128)(2,1)} %shard_map.91) | data formatting | bytes 983040

commit v5 on v4

--- a/solution.py
+++ b/solution.py
@@ -66,7 +66,7 @@
     q_hbm, k_hbm, v_ref, sk_ref, sv_ref, qg_hbm, kg_hbm, w_hbm, pos_hbm,
     out_ref,
     q_ref, k_ref, qg_ref, kg_ref, w_ref, pos_ref,
-    qrot, krot, qbuf, kv, osend, obuf,
+    qrot, krot, qbuf, kv, osend, obuf, proj,
     l_sem, q_ssem, kv_ssem, f_ssem, o_ssem, q_rsem, kv_rsem, o_rsem,
 ):
     rep = lax.axis_index("rep")
@@ -262,16 +262,25 @@
             osend.at[row_slice(slot), :], obuf.at[my_hg],
             o_ssem.at[slot], o_rsem.at[my_hg], dp, my_s,
         )
-    for g in range(GROUPS):
-        piece = obuf.at[g]
-        pltpu.make_async_copy(piece, piece, o_rsem.at[g]).wait()
-    attn = jnp.concatenate([obuf[g] for g in range(GROUPS)], axis=1)
     loads[5].wait()
     own_live = pos < live_count
     d_out = out_ref.shape[1]
-    for at in range(0, d_out, 512):
-        tile = jnp.dot(attn, w_ref[:, at : at + 512], preferred_element_type=jnp.float32)
-        out_ref[:, at : at + 512] = jnp.where(own_live, tile, 0.0).astype(jnp.bfloat16)
+    turn = 1 - 2 * (my_hg // (GROUPS // 2))
+    for step in range(GROUPS):
+        g = lax.rem(my_hg + step * turn + GROUPS, GROUPS)
+        piece = obuf.at[g]
+        pltpu.make_async_copy(piece, piece, o_rsem.at[g]).wait()
+        attn = obuf[g]
+        for at in range(0, d_out, 512):
+            tile = jnp.dot(
+                attn, w_ref[col_slice(g), at : at + 512], preferred_element_type=jnp.float32
+            )
+            if step > 0:
+                tile = tile + proj[:, at : at + 512]
+            if step < GROUPS - 1:
+                proj[:, at : at + 512] = tile
+            else:
+                out_ref[:, at : at + 512] = jnp.where(own_live, tile, 0.0).astype(jnp.bfloat16)
     for copy in forwards:
         copy.wait_send()
     for away, remote in pending:
@@ -307,6 +316,7 @@
             pltpu.VMEM((4, n_patch * rows, width), jnp.bfloat16),
             pltpu.VMEM((per_core * rows, width), jnp.bfloat16),
             pltpu.VMEM((GROUPS, rows, width), jnp.bfloat16),
+            pltpu.VMEM((rows, o_weight.shape[1]), jnp.float32),
             pltpu.SemaphoreType.DMA((6,)),
             pltpu.SemaphoreType.DMA((GROUPS,)),
             pltpu.SemaphoreType.DMA((4, GROUPS * n_chunk)),

time: 47.3 us -> 46.5 us (0.983)
  Pallas kernels: 45.3 us -> 44.5 us
    pallas_call x1, Pallas kernels: 45.3 us -> 44.5 us  [body(): pl.pallas_call(functools.partial(kernel, n_patch, heads, head_dim, rows),...]
where the time goes in v5:
time: 46.5 us; the launch traced here: 46.3 us
  Pallas kernels  44.5 us (96%)
  local copies, waits for them, and re-layouts  1.84 us (4%)
    pallas_call x1, Pallas kernels, body(): pl.pallas_call(functools.partial(kernel, n_patch, heads, head_dim, rows),...  44.5 us
    unnamed x1, local copies, waits for them, and re-layouts  1.84 us

profile of v5, /device:TPU:14, one launch (start us, length us, event | category | flops | bytes accessed | tf_op | source)
XLA Modules:
  0.0 46.3 jit_solution(3501213558045126028)
XLA Ops:
  0.0 44.5 %shard_map.91 = bf16[80,3072]{1,0:T(8,128)(2,1)} custom-call(bf16[80,1536]{1,0:T(8,128)(2,1)} %q_hbm.1, bf16[80,1536]{1,0:T(8,128)(2,1)} %k_hbm.1, bf16[80,1536]{1,0:T(8,128)(2,1)} %v_ref.1, bf16[80,1536]{1,0:T(8,128)(2,1)} %sk_ref.1, bf16[80,1536]{1,0:T(8,128)(2,1)} %sv_ref.1, f32[1,128]{1,0:T(1,128)} %bitcast.2, f32[1,128]{1,0:T(1,128)} %bitcast.3, ...), custom_call_target="tpu_custom_call" | custom-call | tf_op jit(solution)/shard_map/pallas_call | solution.py:301
  44.5 1.8 %copy.11 = bf16[80,3072]{1,0:T(8,128)(2,1)} copy(bf16[80,3072]{1,0:T(8,128)(2,1)} %shard_map.91) | data formatting | bytes 983040
